TPU v7x, 256 devices: a whole 4x4x8 slice. The times are simulated.
256 devices in a mesh: shard: 16 (over x, z_hi, core), rep: 16 (over y, z_lo).
Axes of the slice: x: 4, y: 4, z: 8 (z_hi: 2, z_lo: 4; z = z_hi * 4 + z_lo), core: 2. Of those that a mesh axis runs over, the one named last changes fastest.
Arguments:
- grads: bfloat16 [16, 16, 2097152], P('shard', 'rep'), may hold values from -5000 to 5000
- momentum_codes: int32 [2097152], P(('shard', 'rep')), may hold values from -127 to 127
- variance_codes: int32 [2097152], P(('shard', 'rep')), may hold values from 16 to 255
- momentum_scale: float32 [1280], P(('shard', 'rep')), may hold values from 0.5 to 4, as said below
- variance_scale: float32 [1280], P(('shard', 'rep')), may hold values from 1 to 4, as said below
- master: float32 [2097152], P(('shard', 'rep')), may hold values from -2.5 to 2.5
- step: int32 [1], replicated, may hold values from 1 to 19
Outputs:
- new_master: float32 [2097152], P(('shard', 'rep'))
- weights: bfloat16 [2097152], P('shard')
- update: float32 [2097152], P(('shard', 'rep'))
- momentum_norm: float32 [2097152], P(('shard', 'rep'))
- variance_norm: float32 [2097152], P(('shard', 'rep'))
- momentum_absmax: float32 [1280], P(('shard', 'rep'))
- variance_absmax: float32 [1280], P(('shard', 'rep'))
Inputs may be any that keep to these rules, and one draw needn't show every extreme that they name: `momentum_scale`: A block touched by two neighbouring devices has the same value in both devices' slots. `variance_scale`: A block touched by two neighbouring devices has the same value in both devices' slots.
All inputs are finite; a program needn't handle non-finite values.
Results may differ from a plain program's by a relative error of at most 0.0004.
Values may be sent and summed in bfloat16 or wider, within the bound.
A program may use at most 64 MiB of HBM per device.

v0:
```python
import jax
import jax.numpy as jnp
from jax import lax
from jax.sharding import PartitionSpec as P

BLOCK = 2048


def extended(block, sides, width):
    for axis, dim in sides:
        count = lax.axis_size(axis)
        forward = [(i, i + 1) for i in range(count - 1)]
        backward = [(target, source) for source, target in forward]
        low = lax.ppermute(
            lax.slice_in_dim(block, block.shape[dim] - width, None, axis=dim), axis, forward
        )
        high = lax.ppermute(lax.slice_in_dim(block, 0, width, axis=dim), axis, backward)
        block = jnp.concatenate([low, block, high], axis=dim)
    return block


def on_device(grads, momentum_codes, variance_codes, momentum_scale, variance_scale, master, step):
    own_len = master.shape[0]
    slot_count = momentum_scale.shape[0]
    block_len = BLOCK
    half_len = block_len // 2
    shard_count = lax.axis_size("shard")
    rep_count = lax.axis_size("rep")
    grad_terms = grads.reshape(-1).astype(jnp.float32)
    partial_sum = lax.psum_scatter(grad_terms, "shard", scatter_dimension=0, tiled=True)
    gsum = lax.psum_scatter(partial_sum, "rep", scatter_dimension=0, tiled=True)
    norm_sq = lax.psum(jnp.sum(gsum * gsum), ("shard", "rep"))
    total_params = own_len * shard_count * rep_count
    clip_factor = jnp.minimum(1.0, float(total_params) ** 0.5 / (jnp.sqrt(norm_sq) + 1e-06))
    scaled = gsum * clip_factor

    def spread(scale_table):
        return jnp.repeat(scale_table, block_len)[half_len : half_len + own_len]

    m_old = momentum_codes.astype(jnp.float32) / 127.0 * spread(momentum_scale)
    v_old = variance_codes.astype(jnp.float32) / 255.0 * spread(variance_scale)
    momentum = 0.9 * m_old + 0.1 * scaled
    variance = 0.95 * v_old + 0.05 * scaled * scaled
    count = step[0].astype(jnp.float32)
    first_fix = 1.0 - jnp.power(jnp.float32(0.9), count)
    second_fix = 1.0 - jnp.power(jnp.float32(0.95), count)
    update = momentum / first_fix / (jnp.sqrt(variance / second_fix) + 1e-08)
    new_master = master * (1.0 - 0.0001 * 0.1) - 0.0001 * update
    weights = lax.all_gather(new_master.astype(jnp.bfloat16), "rep", axis=0, tiled=True)

    def slot_max(values):
        padded = jnp.pad(jnp.abs(values), (half_len, half_len))
        return jnp.max(padded.reshape(slot_count, block_len), axis=1)

    m_table = slot_max(momentum)
    v_table = slot_max(variance)
    own_edge = jnp.stack(
        [jnp.stack([m_table[0], v_table[0]]), jnp.stack([m_table[-1], v_table[-1]])]
    )
    rim_vals = extended(own_edge, ((("shard", "rep"), 0),), 1)
    m_table = m_table.at[0].max(rim_vals[0, 0]).at[-1].max(rim_vals[3, 0])
    v_table = v_table.at[0].max(rim_vals[0, 1]).at[-1].max(rim_vals[3, 1])
    momentum_norm = momentum / (spread(m_table) + 1e-06)
    variance_norm = variance / (spread(v_table) + 1e-06)
    return (new_master, weights, update, momentum_norm, variance_norm, m_table, v_table)


def solution(mesh):
    in_specs = (
        P("shard", "rep", None),
        P(("shard", "rep")),
        P(("shard", "rep")),
        P(("shard", "rep")),
        P(("shard", "rep")),
        P(("shard", "rep")),
        P(),
    )
    out_specs = (
        P(("shard", "rep")),
        P("shard"),
        P(("shard", "rep")),
        P(("shard", "rep")),
        P(("shard", "rep")),
        P(("shard", "rep")),
        P(("shard", "rep")),
    )
    return jax.shard_map(
        on_device, mesh=mesh, in_specs=in_specs, out_specs=out_specs, check_vma=False
    )
```

profile of v0, /device:TPU:1, one launch (start us, length us, event | category | flops | bytes accessed | tf_op | source)
XLA Modules:
  0.0 710.2 jit_solution(4956482309576053359)
XLA Ops:
  7.2 10.8 %convert_element_type.28 = f32[1,1,2097152]{2,1,0:T(1,128)} convert(bf16[1,1,2097152]{2,1,0:T(2,128)(2,1)} %param.15) | non-fusion elementwise | flops 2097152 | bytes 12582912 | tf_op jit(solution)/shard_map/convert_element_type | solution.py:29
  20.0 381.4 %all-reduce.7.cloned.1.call-done = f32[2097152]{0:T(1024)} async-done(((f32[2097152]{0:T(1024)}), f32[2097152]{0:T(1024)}) %all-reduce.7.cloned.1.call-update) | async-done | bytes 8388624
  401.3 1.9 dynamic-slice.25
  403.3 0.6 dynamic-slice.26
  405.5 150.3 %all-reduce.9.cloned.1.call-done = f32[131072]{0:T(1024)} async-done(((f32[131072]{0:T(1024)}), f32[131072]{0:T(1024)}) %all-reduce.9.cloned.1.call-update) | async-done | bytes 524304
  555.7 1.4 multiply_reduce_fusion
  557.1 85.7 %psum.7 = f32[]{:T(128)} all-reduce(f32[]{:T(128)} %multiply_reduce_fusion), channel_id=1, replica_groups=mesh['shard'=16,'rep'=16] {'shard','rep'}, use_global_device_ids=true, to_apply=%region_3.0 | all-reduce | flops 1 | bytes 8 | tf_op jit(solution)/shard_map/psum | solution.py:32
  643.5 0.8 fusion.6
  644.5 0.6 slice.84
  645.2 0.6 slice.83
  645.8 1.4 maximum_bitcast_fusion
  647.2 1.9 collective-permute-start
  649.1 6.8 collective-permute-done
  655.9 0.6 fusion.12
  656.5 1.8 constant_dynamic-update-slice_fusion.2
  658.3 1.4 maximum_bitcast_fusion.1
  659.7 2.0 collective-permute-start.1
  661.7 2.3 collective-permute-done.1
  664.0 0.6 fusion.11
  664.6 0.8 constant_dynamic-update-slice_fusion
  665.4 0.8 constant_dynamic-update-slice_fusion.1
  666.4 0.7 fusion.10
  667.0 35.6 %all_gather.3 = bf16[131072]{0:T(1024)(128)(2,1)S(1)} all-gather(bf16[8192]{0:T(1024)(128)(2,1)S(1)} %get-tuple-element.59), channel_id=1, replica_groups=mesh['shard'=16,'rep'=16] {'rep'}, dimensions={0}, use_global_device_ids=true | all-gather | bytes 278528 | tf_op jit(solution)/shard_map/all_gather | solution.py:49
  702.7 0.7 copy.22
  (37 shorter events, 1.9 us)
Async XLA Ops:
  7.2 394.2 %all-reduce.7.cloned.1.call-start = ((), (), s32[]{:S(2)}) async-start(), calls=%async_computation | async-start | bytes 16777216
  18.1 0.7 copy-start.8
  18.1 385.2 %copy-start.7 = (u32[256]{0:T(256)S(1)}, u32[256]{0:T(256)}, u32[]{:S(2)}) copy-start(u32[256]{0:T(256)} %constant.134) | copy-start | bytes 3076
  18.1 385.8 %copy-start.5 = (f32[5]{0:T(128)S(1)}, f32[5]{0:T(128)}, u32[]{:S(2)}) copy-start(f32[5]{0:T(128)} %param.19) | copy-start | bytes 64
  18.1 385.9 %copy-start.6 = (f32[5]{0:T(128)S(1)}, f32[5]{0:T(128)}, u32[]{:S(2)}) copy-start(f32[5]{0:T(128)} %param.18) | copy-start | bytes 64
  18.1 625.4 %copy-start = (s32[8192]{0:T(1024)S(1)}, s32[8192]{0:T(1024)}, u32[]{:S(2)}) copy-start(s32[8192]{0:T(1024)} %param.17) | copy-start | bytes 98308
  18.1 625.4 %copy-start.1 = (s32[8192]{0:T(1024)S(1)}, s32[8192]{0:T(1024)}, u32[]{:S(2)}) copy-start(s32[8192]{0:T(1024)} %param.16) | copy-start | bytes 98308
  18.1 648.2 %copy-start.2 = (f32[8192]{0:T(1024)S(1)}, f32[8192]{0:T(1024)}, u32[]{:S(2)}) copy-start(f32[8192]{0:T(1024)} %param.20) | copy-start | bytes 98308
  18.2 537.6 %all-reduce.9.cloned.1.call-start = ((), (), s32[]{:S(2)}) async-start(), calls=%async_computation.1 | async-start | bytes 1048576
  647.2 8.8 %collective-permute-start = (f32[1,2]{1,0:T(1,128)S(1)}, f32[1,2]{1,0:T(1,128)S(1)}, u32[]{:S(2)}, u32[]{:S(2)}) collective-permute-start(f32[1,2]{1,0:T(1,128)S(1)} %maximum_bitcast_fusion), channel_id=1, source_target_pairs={{0,1},{1,2},{2,3},{3,4},{4,5},{5,6},{6,7},{7,8},{8,9},{9,10},{10,1... | collective-permute-start | bytes 32 | tf_op jit(solution)/shard_map/ppermute | solution.py:14
  659.7 4.3 collective-permute-start.1
  665.4 38.1 %copy-start.3 = (f32[5]{0:T(128)}, f32[5]{0:T(128)S(1)}, u32[]{:S(2)}) copy-start(f32[5]{0:T(128)S(1)} %constant_dynamic-update-slice_fusion) | copy-start | bytes 64
  666.2 37.2 %copy-start.4 = (f32[5]{0:T(128)}, f32[5]{0:T(128)S(1)}, u32[]{:S(2)}) copy-start(f32[5]{0:T(128)S(1)} %constant_dynamic-update-slice_fusion.1) | copy-start | bytes 64
Sparse Core Ops, SparseCore 0:
  18.3 383.0 all-reduce.6
  404.0 151.7 all-reduce.8
where the time goes:
time: 717 us; the launch traced here: 710 us
  waiting for transfers between devices  541 us (75%)
  blocking collectives  121 us (17%)
  other arithmetic  20.1 us (3%)
  between operations  17 us (2%)
    unnamed x4, waiting for transfers between devices  532 us
    psum x1, blocking collectives, on_device(): norm_sq = lax.psum(jnp.sum(gsum * gsum), ('shard', 'rep'))  85.7 us
    all_gather x1, blocking collectives, on_device(): lax.all_gather(new_master.astype(jnp.bfloat16), 'rep', axis=0, tiled=True)  35.6 us
  transfers between devices with their start and end apart: 4, of which 4 were waited for; matrix products, arithmetic and copies ran while one was open for 0% of the time, Pallas kernels for 0%

commit v1 on v0

v1 whole, which is shorter than its diff:
```python
import functools
import math

import jax
import jax.numpy as jnp
from jax import lax
from jax.experimental import pallas as pl
from jax.experimental.pallas import tpu as pltpu
from jax.sharding import PartitionSpec as P

MESH = pl.DeviceIdType.MESH
F32 = jnp.float32
BF16 = jnp.bfloat16

NX, NY, NZ = 4, 4, 8
ROWS = 64
PART_ROWS = (24, 24, 16)
RA, RB, RC = PART_ROWS
TOTAL = float(NX * NY * NZ * 2 * ROWS * 128)
GROUP = 131072
GROUP_ROWS = GROUP // 128

X_OFFSETS = (2, 1, 3, 0)
XY_PEERS = [(dx, dy) for dx in range(NX) for dy in range(NY) if dx or dy]
ZC_PEERS = [(dz, dc) for dz in range(NZ) for dc in range(2) if dz or dc]
REP_PEERS = [(dy, dl) for dy in range(4) for dl in range(4) if dy or dl]


def ring_sends(n):
    order = []
    for step in range(n // 2):
        order.append((1, n // 2 - step))
        if n // 2 - 1 - step >= 1:
            order.append((0, n // 2 - 1 - step))
    return order


def device(x, y, z, c):
    return ((x * 2 + lax.div(z, 4)) * 2 + c, y * 4 + lax.rem(z, 4))


def add_into(dst, src, rows, tile):
    def body(i, carry):
        at = pl.ds(pl.multiple_of(i * tile, tile), tile)
        dst[at, :] = dst[at, :] + src[at, :]
        return carry

    lax.fori_loop(0, rows // tile, body, 0)


def kernel(
    g_ref, mcode_ref, vcode_ref, master_ref, mscale_ref, vscale_ref, step_ref,
    new_ref, w_ref, up_ref, mn_ref, vn_ref, am_ref, av_ref,
    raw, pack, got, sa, sb, sc, ra, rb, rc, a2, b2, c2, a3, b3, c3,
    gs, old, n1, n2, n1r, n2r,
    load_sem, core_sem, ring_a, ring_b, ring_c, two_sem, three_a, three_b, three_c,
    edge_sem, norm1_sem, norm2_sem, out_sem,
):
    s, r = lax.axis_index("shard"), lax.axis_index("rep")
    x, c = lax.div(s, 4), lax.rem(s, 2)
    y, zl = lax.div(r, 4), lax.rem(r, 4)
    zh = lax.rem(lax.div(s, 2), 2)
    z = zh * 4 + zl
    o = s * 16 + r

    def rel(dx=0, dy=0, dz=0, dc=0):
        return device(
            lax.rem(x + dx + NX, NX), lax.rem(y + dy + NY, NY), lax.rem(z + dz + NZ, NZ), lax.rem(c + dc, 2)
        )

    def in_rep(dy, dl):
        return (s, lax.rem(y + dy, 4) * 4 + lax.rem(zl + dl, 4))

    def flat(step):
        to = lax.rem(o + step + 256, 256)
        return (lax.div(to, 16), lax.rem(to, 16))

    def remote(src, dst, sems, index, to):
        return pltpu.make_async_remote_copy(
            src_ref=src, dst_ref=dst, send_sem=sems.at[(0,) + index], recv_sem=sems.at[(1,) + index],
            device_id=to, device_id_type=MESH,
        )

    started = []

    def send(src, dst, sems, index, to):
        copy = remote(src, dst, sems, index, to)
        copy.start()
        started.append(copy)
        return copy

    loads = []
    for i in range(8):
        group = lax.rem(x + X_OFFSETS[i // 2], NX) * 2 + i % 2
        for own in (0, 1):
            core = c if own else 1 - c
            at = pl.multiple_of((group * 2 + core) * GROUP, GROUP)
            load = pltpu.make_async_copy(
                g_ref.at[0, :, pl.ds(at, GROUP)], raw.at[:, pl.ds((2 * i + own) * GROUP, GROUP)], load_sem.at[2 * i + own]
            )
            load.start()
            loads.append(load)

    barrier = pltpu.get_barrier_semaphore()
    peers = [rel(dx=dx, dy=dy) for dx, dy in XY_PEERS] + [rel(dz=dz, dc=dc) for dz, dc in ZC_PEERS]
    peers += [in_rep(dy, dl) for dy, dl in REP_PEERS] + [flat(1), flat(-1)]
    for peer in peers:
        pl.semaphore_signal(barrier, inc=1, device_id=peer, device_id_type=MESH)

    for j in range(5):
        low, high = max(16 * j - 8, 0), min(16 * j + 8, ROWS)
        old[0, 8 + low : 8 + high, :] = mcode_ref[low:high, :].astype(F32) / 127.0 * mscale_ref[j]
        old[1, 8 + low : 8 + high, :] = vcode_ref[low:high, :].astype(F32) / 255.0 * vscale_ref[j]

    def pack_group(i):
        loads[2 * i].wait()

        def body(k, carry):
            for u in range(4):
                at = pl.multiple_of(2 * i * GROUP + k * 8192 + u * 2048, 2048)
                pack[i, pl.ds(pl.multiple_of(k * 64 + u * 16, 16), 16), :] = raw[:, pl.ds(at, 2048)].reshape(16, 128)
            return carry

        lax.fori_loop(0, 16, body, 0)

    pack_group(0)
    pl.semaphore_wait(barrier, len(peers))
    edges = [
        send(old.at[:, pl.ds(64, 8), :], old.at[:, pl.ds(0, 8), :], edge_sem, (0,), flat(1)),
        send(old.at[:, pl.ds(8, 8), :], old.at[:, pl.ds(72, 8), :], edge_sem, (1,), flat(-1)),
    ]
    swaps = []
    for i in range(8):
        if i:
            pack_group(i)
        swaps.append(send(pack.at[i], got.at[i], core_sem, (i,), rel(dc=1)))

    rings = (
        (sa, ra, ring_a, NX, x, "dx", RA),
        (sb, rb, ring_b, NY, y, "dy", RB),
        (sc, rc, ring_c, NZ, z, "dz", RC),
    )
    copies = {}

    def ring_step(part, event):
        total, slots, sems, n, here, name, rows = rings[part]
        half = total.shape[1] // 2
        long, k = ring_sends(n)[event]
        for d, step in enumerate((1, -1)):
            which = (0 if long else 1) if d == 0 else (1 if long else 0)
            target = lax.rem(here + step * k + n, n)
            mine = total.at[target, pl.ds(which * half, half), :]
            if (part, d, long, k + 1) in copies:
                copies[part, d, long, k + 1].wait_recv()
                index = [e for e, v in enumerate(ring_sends(n)) if v == (long, k + 1)][0]
                src = slots.at[d, index]
                add_into(src, mine, half, 64)
            else:
                src = mine
            copies[part, d, long, k] = send(src, slots.at[d, event], sems, (d, event), rel(**{name: step}))

    def ring_end(part, long):
        total, slots, sems, n, here, name, rows = rings[part]
        half = total.shape[1] // 2
        index = [e for e, v in enumerate(ring_sends(n)) if v == (long, 1)][0]
        for d in range(2):
            which = (0 if long else 1) if d == 0 else (1 if long else 0)
            copies[part, d, long, 1].wait_recv()
            add_into(total.at[here, pl.ds(which * half, half), :], slots.at[d, index], half, 64)

    for i in range(8):
        group_x = lax.rem(x + X_OFFSETS[i // 2], NX)
        loads[2 * i + 1].wait()
        swaps[i].wait_recv()

        def body(j, carry, i=i, group_x=group_x):
            jy = lax.div(j, 4)
            jz = lax.rem(j, 4) + (i % 2) * 4
            for u in range(4):
                other = got[i, pl.ds(pl.multiple_of(j * 64 + u * 16, 16), 16), :].astype(F32)
                for v in range(2):
                    at = pl.multiple_of((2 * i + 1) * GROUP + j * 8192 + u * 2048 + v * 1024, 1024)
                    row = u * 16 + v * 8
                    both = raw[:, pl.ds(at, 1024)].astype(F32).reshape(8, 128) + other[v * 8 : v * 8 + 8]
                    if row < RA:
                        sa[group_x, pl.ds(pl.multiple_of((jy * NZ + jz) * RA + row, 8), 8), :] = both
                    elif row < RA + RB:
                        sb[jy, pl.ds(pl.multiple_of((group_x * NZ + jz) * RB + row - RA, 8), 8), :] = both
                    else:
                        sc[jz, pl.ds(pl.multiple_of((group_x * NY + jy) * RC + row - RA - RB, 8), 8), :] = both
            return carry

        lax.fori_loop(0, 16, body, 0)
        if i == 1:
            ring_step(0, 0)
        if i == 5:
            ring_step(0, 1)
    ring_step(2, 0)
    ring_step(1, 0)
    ring_step(2, 1)
    ring_step(1, 1)
    ring_step(2, 2)
    ring_step(2, 3)
    ring_step(0, 2)
    ring_step(1, 2)
    ring_step(2, 4)
    ring_step(2, 5)
    ring_step(2, 6)
    ring_end(0, 0)
    ring_end(1, 0)
    ring_end(2, 0)
    ring_end(2, 1)

    def second_send(part, total, here, slots, there, n, name, size):
        out = []
        for d in range(1, n):
            to = lax.rem(there + d, n)
            src = total.at[here, pl.ds(pl.multiple_of(to * size, 8), size), :]
            out.append(send(src, slots.at[d - 1], two_sem, (part, d - 1), rel(**{name: d})))
        return out

    def second_add(waits, total, here, slots, there, n, size):
        for copy in waits:
            copy.wait_recv()

        def body(i, carry):
            at = pl.ds(pl.multiple_of(i * 32, 32), 32)
            own = pl.ds(pl.multiple_of(there * size + i * 32, 8), 32)
            value = total[here, own, :]
            for d in range(n - 1):
                value = value + slots[d, at, :]
            total[here, own, :] = value
            return carry

        lax.fori_loop(0, size // 32, body, 0)

    two_c = second_send(2, sc, z, c2, x, NX, "dx", NY * RC)
    ring_end(0, 1)
    two_a = second_send(0, sa, x, a2, y, NY, "dy", NZ * RA)
    ring_end(1, 1)
    two_b = second_send(1, sb, y, b2, x, NX, "dx", NZ * RB)

    def third_send(total, here, base, slots, sems, there, n, name, size):
        out = []
        for d in range(1, n):
            to = lax.rem(there + d, n)
            src = total.at[here, pl.ds(pl.multiple_of(base + to * size, 8), size), :]
            out.append(send(src, slots.at[d - 1], sems, (d - 1,), rel(**{name: d})))
        return out

    def third_add(waits, total, here, base, slots, there, n, size, row):
        value = total[here, pl.ds(pl.multiple_of(base + there * size, 8), size), :]
        for d, copy in enumerate(waits):
            copy.wait_recv()
            value = value + slots[d]
        gs[8 + row : 8 + row + size, :] = value
        square = value * value
        return sum(square[8 * q : 8 * q + 8] for q in range(size // 8))

    second_add(two_c, sc, z, c2, x, NX, NY * RC)
    three_cs = third_send(sc, z, x * (NY * RC), c3, three_c, y, NY, "dy", RC)
    second_add(two_a, sa, x, a2, y, NY, NZ * RA)
    three_as = third_send(sa, x, y * (NZ * RA), a3, three_a, z, NZ, "dz", RA)
    second_add(two_b, sb, y, b2, x, NX, NZ * RB)
    three_bs = third_send(sb, y, x * (NZ * RB), b3, three_b, z, NZ, "dz", RB)
    square = third_add(three_cs, sc, z, x * (NY * RC), c3, y, NY, RC, RA + RB)
    square = square + third_add(three_as, sa, x, y * (NZ * RA), a3, z, NZ, RA, 0)
    square = square + third_add(three_bs, sb, y, x * (NZ * RB), b3, z, NZ, RB, RA)

    n1[...] = square
    norm1 = [
        send(n1, n1r.at[i], norm1_sem, (i,), rel(dx=dx, dy=dy)) for i, (dx, dy) in enumerate(XY_PEERS)
    ]
    rims = [
        send(gs.at[pl.ds(64, 8), :], gs.at[pl.ds(0, 8), :], edge_sem, (2,), flat(1)),
        send(gs.at[pl.ds(8, 8), :], gs.at[pl.ds(72, 8), :], edge_sem, (3,), flat(-1)),
    ]
    for i, copy in enumerate(norm1):
        copy.wait_recv()
        square = square + n1r[i]
    n2[...] = square
    norm2 = [
        send(n2, n2r.at[i], norm2_sem, (i,), rel(dz=dz, dc=dc)) for i, (dz, dc) in enumerate(ZC_PEERS)
    ]
    count = jnp.full((8, 128), step_ref[0].astype(F32), F32)
    first_fix = 1.0 - jnp.exp(count * math.log(0.9))
    second_fix = 1.0 - jnp.exp(count * math.log(0.95))
    for copy in edges + rims:
        copy.wait_recv()
    for i, copy in enumerate(norm2):
        copy.wait_recv()
        square = square + n2r[i]
    norm = jnp.sqrt(jnp.full((8, 128), jnp.sum(square), F32))
    clip = jnp.minimum(1.0, TOTAL**0.5 / (norm + 1e-06))

    def moments(row):
        scaled = gs[row : row + 8, :] * clip
        momentum = 0.9 * old[0, row : row + 8, :] + 0.1 * scaled
        variance = 0.95 * old[1, row : row + 8, :] + 0.05 * scaled * scaled
        return momentum, variance

    pairs = [moments(8 * q) for q in range(10)]
    for q in range(8):
        momentum, variance = pairs[q + 1]
        update = momentum / first_fix / (jnp.sqrt(variance / second_fix) + 1e-08)
        up_ref[8 * q : 8 * q + 8, :] = update
        new_ref[8 * q : 8 * q + 8, :] = master_ref[8 * q : 8 * q + 8, :] * (1.0 - 0.0001 * 0.1) - 0.0001 * update
    own_rows = pl.ds(pl.multiple_of(r * ROWS, ROWS), ROWS)
    w_ref[own_rows, :] = new_ref[...].astype(BF16)
    gathers = [
        send(w_ref.at[own_rows, :], w_ref.at[own_rows, :], out_sem, (i,), in_rep(dy, dl))
        for i, (dy, dl) in enumerate(REP_PEERS)
    ]
    first = (o > 0).astype(F32)
    last = (o < 255).astype(F32)
    for j in range(5):
        (ma, va), (mb, vb) = pairs[2 * j], pairs[2 * j + 1]
        ma, va, mb, vb = jnp.abs(ma), jnp.abs(va), jnp.abs(mb), jnp.abs(vb)
        if j == 0:
            ma, va = ma * first, va * first
        if j == 4:
            mb, vb = mb * last, vb * last
        m_max = jnp.max(jnp.maximum(ma, mb))
        v_max = jnp.max(jnp.maximum(va, vb))
        am_ref[j] = m_max
        av_ref[j] = v_max
        for q in (2 * j - 1, 2 * j):
            if 0 <= q < 8:
                mn_ref[8 * q : 8 * q + 8, :] = pairs[q + 1][0] / (m_max + 1e-06)
                vn_ref[8 * q : 8 * q + 8, :] = pairs[q + 1][1] / (v_max + 1e-06)
    for copy in gathers:
        copy.wait_recv()
    for copy in started:
        copy.wait_send()


def on_device(grads, momentum_codes, variance_codes, momentum_scale, variance_scale, master, step):
    vmem = pl.BlockSpec(memory_space=pltpu.VMEM)
    smem = pl.BlockSpec(memory_space=pltpu.SMEM)
    tile = jax.ShapeDtypeStruct((ROWS, 128), F32)
    dma = pltpu.SemaphoreType.DMA
    new, weights, update, m_norm, v_norm, m_max, v_max = pl.pallas_call(
        kernel,
        out_shape=(
            tile, jax.ShapeDtypeStruct((16 * ROWS, 128), BF16), tile, tile, tile,
            jax.ShapeDtypeStruct((5,), F32), jax.ShapeDtypeStruct((5,), F32),
        ),
        in_specs=[pl.BlockSpec(memory_space=pl.ANY), vmem, vmem, vmem, smem, smem, smem],
        out_specs=(vmem, vmem, vmem, vmem, vmem, smem, smem),
        scratch_shapes=[
            pltpu.VMEM((1, 16 * GROUP), BF16),
            pltpu.VMEM((8, GROUP_ROWS, 128), BF16),
            pltpu.VMEM((8, GROUP_ROWS, 128), BF16),
            pltpu.VMEM((NX, NY * NZ * RA, 128), F32),
            pltpu.VMEM((NY, NX * NZ * RB, 128), F32),
            pltpu.VMEM((NZ, NX * NY * RC, 128), F32),
            pltpu.VMEM((2, 3, NY * NZ * RA // 2, 128), F32),
            pltpu.VMEM((2, 3, NX * NZ * RB // 2, 128), F32),
            pltpu.VMEM((2, 7, NX * NY * RC // 2, 128), F32),
            pltpu.VMEM((NY - 1, NZ * RA, 128), F32),
            pltpu.VMEM((NX - 1, NZ * RB, 128), F32),
            pltpu.VMEM((NX - 1, NY * RC, 128), F32),
            pltpu.VMEM((NZ - 1, RA, 128), F32),
            pltpu.VMEM((NZ - 1, RB, 128), F32),
            pltpu.VMEM((NY - 1, RC, 128), F32),
            pltpu.VMEM((80, 128), F32),
            pltpu.VMEM((2, 80, 128), F32),
            pltpu.VMEM((8, 128), F32),
            pltpu.VMEM((8, 128), F32),
            pltpu.VMEM((15, 8, 128), F32),
            pltpu.VMEM((15, 8, 128), F32),
            dma((16,)), dma((2, 8)), dma((2, 2, 3)), dma((2, 2, 3)), dma((2, 2, 7)), dma((2, 3, 3)),
            dma((2, 7)), dma((2, 7)), dma((2, 3)),
            dma((2, 4)), dma((2, 15)), dma((2, 15)), dma((2, 15)),
        ],
        compiler_params=pltpu.CompilerParams(
            collective_id=0, has_side_effects=True, vmem_limit_bytes=48 * 2**20
        ),
        name="adam_window",
    )(
        grads, momentum_codes.reshape(ROWS, 128), variance_codes.reshape(ROWS, 128), master.reshape(ROWS, 128),
        momentum_scale, variance_scale, step,
    )
    return (
        new.reshape(-1), weights.reshape(-1), update.reshape(-1), m_norm.reshape(-1), v_norm.reshape(-1), m_max, v_max
    )


def solution(mesh):
    own = P(("shard", "rep"))
    return jax.shard_map(
        on_device,
        mesh=mesh,
        in_specs=(P("shard", "rep", None), own, own, own, own, own, P()),
        out_specs=(own, P("shard"), own, own, own, own, own),
        check_vma=False,
    )
```

time: 717 us -> 75.6 us (0.11)
  waiting for transfers between devices: 541 us -> 0 us
  blocking collectives: 121 us -> 0 us
  Pallas kernels: 0 us -> 66.2 us
  other arithmetic: 20.1 us -> 0 us
  between operations: 17 us -> 1.3 us
    unnamed x4 -> x0, waiting for transfers between devices: 532 us -> none
    psum x1 -> x0, blocking collectives: 85.7 us -> none  [on_device(): norm_sq = lax.psum(jnp.sum(gsum * gsum), ('shard', 'rep'))]
    pallas_call x0 -> x1, Pallas kernels: none -> 66.2 us  [on_device(): pl.pallas_call(kernel, out_shape=(tile, jax.ShapeDtypeStruct((16 * ROWS,...]
    all_gather x1 -> x0, blocking collectives: 35.6 us -> none  [on_device(): lax.all_gather(new_master.astype(jnp.bfloat16), 'rep', axis=0, tiled=True)]
    convert_element_type x2 -> x0, other arithmetic: 11.5 us -> none  [the longest x1 10.8 us: on_device(): grad_terms = grads.reshape(-1).astype(jnp.float32)]
    ppermute x2 -> x0, waiting for transfers between devices: 9.13 us -> none  [the longest x1 6.84 us: extended(): lax.ppermute(lax.slice_in_dim(block, block.shape[dim] - width, None, axis...]
  transfers between devices with their start and end apart: 4 -> 0, of which waited for: 4 -> 0; matrix products, arithmetic and copies ran while one was open for 0% -> 0% of each run, Pallas kernels for 0% -> 0%
where the time goes in v1:
time: 75.6 us; the launch traced here: 75.3 us
  Pallas kernels  66.2 us (88%)
  local copies, waits for them, and re-layouts  7.79 us (10%)
  between operations  1.3 us (2%)
    pallas_call x1, Pallas kernels, on_device(): pl.pallas_call(kernel, out_shape=(tile, jax.ShapeDtypeStruct((16 * ROWS,...  66.2 us
    unnamed x17, local copies, waits for them, and re-layouts  7.79 us

profile of v1, /device:TPU:1, one launch (start us, length us, event | category | flops | bytes accessed | tf_op | source)
XLA Modules:
  0.0 75.3 jit_solution(633872162193557274)
XLA Ops:
  1.3 0.0 copy-start
  1.3 0.7 copy-done
  2.0 0.0 copy-start.1
  2.0 0.8 %copy-done.1 = s32[8192]{0:T(1024)S(1)} copy-done((s32[8192]{0:T(1024)S(1)}, s32[8192]{0:T(1024)}, u32[]{:S(2)}) %copy-start.1) | copy-done | bytes 32792
  2.8 0.0 copy-start.2
  2.8 0.8 %copy-done.2 = f32[8192]{0:T(1024)S(1)} copy-done((f32[8192]{0:T(1024)S(1)}, f32[8192]{0:T(1024)}, u32[]{:S(2)}) %copy-start.2) | copy-done | bytes 32792
  3.6 0.0 copy-start.3
  3.6 0.7 copy-done.3
  4.2 0.0 copy-start.4
  4.2 0.7 copy-done.4
  4.9 66.2 %adam_window.1 = (f32[64,128]{1,0:T(8,128)S(1)}, bf16[1024,128]{1,0:T(8,128)(2,1)S(1)}, f32[64,128]{1,0:T(8,128)S(1)}, f32[64,128]{1,0:T(8,128)S(1)}, f32[64,128...) custom-call(bf16[1,1,2097152]{2,1,0:T(2,128)(2,1)} %g_ref.1, s32[64,128]{1,0:T(8,128)S(1)} %bitcast.9, ...), custom_call_target="tpu_custom_call" | custom-call | tf_op jit(solution)/shard_map/adam_window/pallas_call | solution.py:342
  71.1 0.6 copy.22
  71.7 0.7 copy.23
  72.4 0.6 copy.24
  73.0 0.6 copy.25
  73.6 0.6 copy.26
  74.3 0.5 copy.27
  74.8 0.5 copy.28
Async XLA Ops:
  1.3 0.8 %copy-start = (s32[8192]{0:T(1024)S(1)}, s32[8192]{0:T(1024)}, u32[]{:S(2)}) copy-start(s32[8192]{0:T(1024)} %param.8) | copy-start | bytes 98308
  2.0 0.8 %copy-start.1 = (s32[8192]{0:T(1024)S(1)}, s32[8192]{0:T(1024)}, u32[]{:S(2)}) copy-start(s32[8192]{0:T(1024)} %param.9) | copy-start | bytes 98308
  2.8 0.8 %copy-start.2 = (f32[8192]{0:T(1024)S(1)}, f32[8192]{0:T(1024)}, u32[]{:S(2)}) copy-start(f32[8192]{0:T(1024)} %param.12) | copy-start | bytes 98308
  3.6 0.7 copy-start.3
  4.2 0.7 copy-start.4

commit v2 on v1

--- a/solution.py
+++ b/solution.py
@@ -102,8 +102,7 @@
             loads.append(load)
 
     barrier = pltpu.get_barrier_semaphore()
-    peers = [rel(dx=dx, dy=dy) for dx, dy in XY_PEERS] + [rel(dz=dz, dc=dc) for dz, dc in ZC_PEERS]
-    peers += [in_rep(dy, dl) for dy, dl in REP_PEERS] + [flat(1), flat(-1)]
+    peers = [rel(dc=1), rel(dx=1), rel(dx=-1), rel(dy=1), rel(dy=-1), rel(dz=1), rel(dz=-1)]
     for peer in peers:
         pl.semaphore_signal(barrier, inc=1, device_id=peer, device_id_type=MESH)
 
@@ -125,10 +124,6 @@
 
     pack_group(0)
     pl.semaphore_wait(barrier, len(peers))
-    edges = [
-        send(old.at[:, pl.ds(64, 8), :], old.at[:, pl.ds(0, 8), :], edge_sem, (0,), flat(1)),
-        send(old.at[:, pl.ds(8, 8), :], old.at[:, pl.ds(72, 8), :], edge_sem, (1,), flat(-1)),
-    ]
     swaps = []
     for i in range(8):
         if i:
@@ -270,6 +265,10 @@
     n1[...] = square
     norm1 = [
         send(n1, n1r.at[i], norm1_sem, (i,), rel(dx=dx, dy=dy)) for i, (dx, dy) in enumerate(XY_PEERS)
+    ]
+    edges = [
+        send(old.at[:, pl.ds(64, 8), :], old.at[:, pl.ds(0, 8), :], edge_sem, (0,), flat(1)),
+        send(old.at[:, pl.ds(8, 8), :], old.at[:, pl.ds(72, 8), :], edge_sem, (1,), flat(-1)),
     ]
     rims = [
         send(gs.at[pl.ds(64, 8), :], gs.at[pl.ds(0, 8), :], edge_sem, (2,), flat(1)),

time: 75.6 us -> 72.2 us (0.955)
  Pallas kernels: 66.2 us -> 62.8 us
    pallas_call x1, Pallas kernels: 66.2 us -> 62.8 us  [on_device(): pl.pallas_call(kernel, out_shape=(tile, jax.ShapeDtypeStruct((16 * ROWS,...]
where the time goes in v2:
time: 72.2 us; the launch traced here: 71.9 us
  Pallas kernels  62.8 us (87%)
  local copies, waits for them, and re-layouts  7.79 us (11%)
  between operations  1.3 us (2%)
    pallas_call x1, Pallas kernels, on_device(): pl.pallas_call(kernel, out_shape=(tile, jax.ShapeDtypeStruct((16 * ROWS,...  62.8 us
    unnamed x17, local copies, waits for them, and re-layouts  7.79 us

profile of v2, /device:TPU:1, one launch (start us, length us, event | category | flops | bytes accessed | tf_op | source)
XLA Modules:
  0.0 71.9 jit_solution(2350065821220212832)
XLA Ops:
  1.3 0.0 copy-start
  1.3 0.7 %copy-done = s32[8192]{0:T(1024)S(1)} copy-done((s32[8192]{0:T(1024)S(1)}, s32[8192]{0:T(1024)}, u32[]{:S(2)}) %copy-start) | copy-done | bytes 32792
  2.0 0.0 copy-start.1
  2.0 0.8 %copy-done.1 = s32[8192]{0:T(1024)S(1)} copy-done((s32[8192]{0:T(1024)S(1)}, s32[8192]{0:T(1024)}, u32[]{:S(2)}) %copy-start.1) | copy-done | bytes 32792
  2.8 0.0 copy-start.2
  2.8 0.8 %copy-done.2 = f32[8192]{0:T(1024)S(1)} copy-done((f32[8192]{0:T(1024)S(1)}, f32[8192]{0:T(1024)}, u32[]{:S(2)}) %copy-start.2) | copy-done | bytes 32792
  3.6 0.0 copy-start.3
  3.6 0.7 copy-done.3
  4.2 0.0 copy-start.4
  4.2 0.7 copy-done.4
  4.9 62.8 %adam_window.1 = (f32[64,128]{1,0:T(8,128)S(1)}, bf16[1024,128]{1,0:T(8,128)(2,1)S(1)}, f32[64,128]{1,0:T(8,128)S(1)}, f32[64,128]{1,0:T(8,128)S(1)}, f32[64,128...) custom-call(bf16[1,1,2097152]{2,1,0:T(2,128)(2,1)} %g_ref.1, s32[64,128]{1,0:T(8,128)S(1)} %bitcast.9, ...), custom_call_target="tpu_custom_call" | custom-call | tf_op jit(solution)/shard_map/adam_window/pallas_call | solution.py:341
  67.7 0.6 copy.22
  68.3 0.7 %copy.23 = bf16[131072]{0:T(1024)(128)(2,1)} copy(bf16[131072]{0:T(1024)(128)(2,1)S(1)} %bitcast.8) | data formatting | bytes 524288
  69.0 0.6 copy.24
  69.6 0.6 copy.25
  70.2 0.6 copy.26
  70.9 0.5 copy.27
  71.4 0.5 copy.28
Async XLA Ops:
  1.3 0.8 %copy-start = (s32[8192]{0:T(1024)S(1)}, s32[8192]{0:T(1024)}, u32[]{:S(2)}) copy-start(s32[8192]{0:T(1024)} %param.8) | copy-start | bytes 98308
  2.0 0.8 %copy-start.1 = (s32[8192]{0:T(1024)S(1)}, s32[8192]{0:T(1024)}, u32[]{:S(2)}) copy-start(s32[8192]{0:T(1024)} %param.9) | copy-start | bytes 98308
  2.8 0.8 %copy-start.2 = (f32[8192]{0:T(1024)S(1)}, f32[8192]{0:T(1024)}, u32[]{:S(2)}) copy-start(f32[8192]{0:T(1024)} %param.12) | copy-start | bytes 98308
  3.6 0.7 copy-start.3
  4.2 0.7 copy-start.4

commit v3 on v0

v3 whole, which is shorter than its diff:
```python
import math

import jax
import jax.numpy as jnp
from jax import lax
from jax.experimental import pallas as pl
from jax.experimental.pallas import tpu as pltpu
from jax.sharding import PartitionSpec as P

MESH = pl.DeviceIdType.MESH
F32 = jnp.float32
BF16 = jnp.bfloat16

NX, NY, NZ = 4, 4, 8
SIZES = {"x": NX, "y": NY, "z": NZ, "c": 2}
ROWS = 64
TOTAL = float(NX * NY * NZ * 2 * ROWS * 128)
GROUP = 131072
GROUP_ROWS = GROUP // 128

PARTS = (("xyz", 0, 16), ("yxz", 16, 16), ("zxy", 32, 16), ("xyz", 48, 8), ("yxz", 56, 8))

X_OFFSETS = (2, 1, 3, 0)
PLACE = {d: i for i, d in enumerate(X_OFFSETS)}


XY_PEERS = ((2, 2), (1, 2), (2, 1), (2, 3), (3, 2), (0, 2), (1, 1), (1, 3), (2, 0), (3, 1), (3, 3), (0, 1), (0, 3), (1, 0), (3, 0))
ZC_PEERS = ((4, 1), (4, 0), (3, 1), (5, 1), (3, 0), (5, 0), (2, 1), (6, 1), (2, 0), (6, 0), (1, 1), (7, 1), (1, 0), (7, 0), (0, 1))
REP_PEERS = ((2, 3), (1, 3), (2, 2), (3, 3), (0, 3), (1, 2), (2, 1), (3, 2), (0, 2), (1, 1), (2, 0), (3, 1), (0, 1), (1, 0), (3, 0))
FAR_FIRST = {4: (2, 1, 3), 8: (4, 3, 5, 2, 6, 1, 7)}


def ring_sends(n):
    order = []
    for step in range(n // 2):
        order.append((1, n // 2 - step))
        if n // 2 - 1 - step >= 1:
            order.append((0, n // 2 - 1 - step))
    return order


def half_of(d, long):
    return 1 - long if d == 0 else long


PACK, SUM, RING, END, SECOND, THIRD, LAST = range(7)
ORDER = (
    (PACK, 0), (PACK, 1), (PACK, 2), (PACK, 3), (PACK, 4), (SUM, 0), (PACK, 5), (PACK, 6), (PACK, 7), (SUM, 1),
    (RING, 0, 0, 1, 2), (RING, 0, 1, 1, 2), (RING, 3, 0, 1, 2), (RING, 3, 1, 1, 2), (SUM, 2), (SUM, 3),
    (RING, 0, 0, 0, 1), (RING, 1, 0, 1, 2), (RING, 1, 1, 0, 1), (RING, 2, 0, 1, 4), (RING, 2, 1, 0, 3),
    (RING, 3, 0, 0, 1), (RING, 4, 0, 1, 2), (RING, 4, 1, 0, 1), (SUM, 4), (SUM, 5), (RING, 0, 1, 0, 1),
    (RING, 3, 1, 0, 1), (SUM, 6), (SUM, 7), (RING, 1, 0, 0, 1), (RING, 1, 1, 1, 2), (RING, 2, 0, 0, 3),
    (RING, 2, 1, 1, 4), (RING, 4, 0, 0, 1), (RING, 4, 1, 1, 2), (RING, 0, 0, 1, 1), (RING, 0, 1, 1, 1),
    (RING, 2, 0, 1, 3), (RING, 2, 1, 0, 2), (RING, 3, 0, 1, 1), (RING, 1, 0, 1, 1), (RING, 3, 1, 1, 1),
    (END, 1, 1, 0), (RING, 4, 0, 1, 1), (END, 4, 1, 0), (RING, 2, 0, 0, 2), (RING, 2, 1, 1, 3), (END, 0, 0, 0),
    (END, 0, 1, 0), (RING, 2, 0, 1, 2), (RING, 2, 1, 0, 1), (END, 3, 0, 0), (END, 1, 0, 0), (END, 3, 1, 0),
    (RING, 1, 1, 1, 1), (RING, 2, 0, 0, 1), (RING, 2, 1, 1, 2), (END, 4, 0, 0), (RING, 4, 1, 1, 1),
    (RING, 2, 0, 1, 1), (END, 2, 1, 0), (END, 0, 0, 1), (END, 0, 1, 1), (SECOND, 0), (END, 3, 0, 1), (END, 1, 0, 1),
    (END, 3, 1, 1), (SECOND, 3), (END, 2, 0, 0), (RING, 2, 1, 1, 1), (END, 1, 1, 1), (SECOND, 1), (END, 4, 0, 1),
    (END, 2, 0, 1), (END, 4, 1, 1), (SECOND, 4), (END, 2, 1, 1), (SECOND, 2), (THIRD, 0), (THIRD, 1), (THIRD, 3),
    (THIRD, 4), (THIRD, 2), (LAST, 0), (LAST, 2), (LAST, 1), (LAST, 3), (LAST, 4),
)


def device(x, y, z, c):
    return ((x * 2 + lax.div(z, 4)) * 2 + c, y * 4 + lax.rem(z, 4))


def add_into(dst, src, rows, tile=64):
    def body(i, carry):
        at = pl.ds(pl.multiple_of(i * tile, tile), tile)
        dst[at, :] = dst[at, :] + src[at, :]
        return carry

    lax.fori_loop(0, rows // tile, body, 0)


def layout():
    dma = pltpu.SemaphoreType.DMA
    out = {
        "raw": pltpu.VMEM((1, 16 * GROUP), BF16),
        "pack": pltpu.VMEM((8, GROUP_ROWS, 128), BF16),
        "got": pltpu.VMEM((8, GROUP_ROWS, 128), BF16),
        "mcode": pltpu.VMEM((ROWS, 128), jnp.int32),
        "vcode": pltpu.VMEM((ROWS, 128), jnp.int32),
        "master": pltpu.VMEM((ROWS, 128), F32),
        "mscale": pltpu.SMEM((5,), F32),
        "vscale": pltpu.SMEM((5,), F32),
        "step": pltpu.SMEM((1,), jnp.int32),
        "state": pltpu.VMEM((3, 80, 128), F32),
        "out": pltpu.VMEM((4, ROWS, 128), F32),
        "half": pltpu.VMEM((ROWS, 128), BF16),
        "am": pltpu.SMEM((5,), F32),
        "av": pltpu.SMEM((5,), F32),
        "n1": pltpu.VMEM((8, 128), F32),
        "n2": pltpu.VMEM((8, 128), F32),
        "n1r": pltpu.VMEM((15, 8, 128), F32),
        "n2r": pltpu.VMEM((15, 8, 128), F32),
        "load_sem": dma((16,)),
        "input_sem": dma((6,)),
        "core_sem": dma((2, 8)),
        "edge_sem": dma((2, 2)),
        "norm1_sem": dma((2, 15)),
        "norm2_sem": dma((2, 15)),
        "out_sem": dma((2, 15)),
        "leave_sem": dma((7,)),
    }
    for p, (axes, _, rows) in enumerate(PARTS):
        n1, n2, n3 = (SIZES[a] for a in axes)
        out["sum", p] = pltpu.VMEM((n1, n2 * n3 * rows, 128), F32)
        out["ring", p] = pltpu.VMEM((2, n1 - 1, n2 * n3 * rows // 2, 128), F32)
        out["two", p] = pltpu.VMEM((n2 - 1, n3 * rows, 128), F32)
        out["three", p] = pltpu.VMEM((n3 - 1, rows, 128), F32)
        out["ring_sem", p] = dma((2, 2, n1 - 1))
        out["two_sem", p] = dma((2, n2 - 1))
        out["three_sem", p] = dma((2, n3 - 1))
    return out


def kernel(g_ref, mcode_ref, vcode_ref, mscale_ref, vscale_ref, master_ref, step_ref, new_hbm, w_ref, up_hbm, mn_hbm, vn_hbm, am_hbm, av_hbm, *scratches):
    refs = {}
    for name, ref in zip(layout(), scratches):
        refs[name] = ref
    raw, pack, got, state = refs["raw"], refs["pack"], refs["got"], refs["state"]
    s, r = lax.axis_index("shard"), lax.axis_index("rep")
    x, c = lax.div(s, 4), lax.rem(s, 2)
    y, zl = lax.div(r, 4), lax.rem(r, 4)
    z = lax.rem(lax.div(s, 2), 2) * 4 + zl
    here = {"x": x, "y": y, "z": z}
    o = s * 16 + r

    def rel(*moves):
        at = {"x": x, "y": y, "z": z, "c": c}
        for axis, by in moves:
            at[axis] = lax.rem(at[axis] + by + SIZES[axis], SIZES[axis])
        return device(at["x"], at["y"], at["z"], at["c"])

    def in_rep(dy, dl):
        return (s, lax.rem(y + dy, 4) * 4 + lax.rem(zl + dl, 4))

    def flat(step):
        to = lax.rem(o + step + 256, 256)
        return (lax.div(to, 16), lax.rem(to, 16))

    started = []

    def send(src, dst, sems, index, to):
        copy = pltpu.make_async_remote_copy(
            src_ref=src, dst_ref=dst, send_sem=sems.at[(0,) + index], recv_sem=sems.at[(1,) + index],
            device_id=to, device_id_type=MESH,
        )
        copy.start()
        started.append(copy)
        return copy

    barrier = pltpu.get_barrier_semaphore()
    peers = [rel(("c", 1))] + [rel((a, d)) for a in "xyz" for d in (1, -1)]
    for peer in peers:
        pl.semaphore_signal(barrier, inc=1, device_id=peer, device_id_type=MESH)

    loads = []
    for i in range(8):
        group = lax.rem(x + X_OFFSETS[i // 2], NX) * 2 + i % 2
        for own in (0, 1):
            core = c if own else 1 - c
            at = pl.multiple_of((group * 2 + core) * GROUP, GROUP)
            load = pltpu.make_async_copy(
                g_ref.at[0, :, pl.ds(at, GROUP)],
                raw.at[:, pl.ds((2 * i + own) * GROUP, GROUP)],
                refs["load_sem"].at[2 * i + own],
            )
            load.start()
            loads.append(load)
    inputs = []
    for i, (src, name) in enumerate(
        (
            (mcode_ref, "mcode"), (vcode_ref, "vcode"), (master_ref, "master"),
            (mscale_ref, "mscale"), (vscale_ref, "vscale"), (step_ref, "step"),
        )
    ):
        copy = pltpu.make_async_copy(src, refs[name], refs["input_sem"].at[i])
        copy.start()
        inputs.append(copy)

    swaps = {}

    def pack_step(i):
        loads[2 * i].wait()

        def body(k, carry):
            for u in range(4):
                at = pl.multiple_of(2 * i * GROUP + k * 8192 + u * 2048, 2048)
                pack[i, pl.ds(pl.multiple_of(k * 64 + u * 16, 16), 16), :] = raw[:, pl.ds(at, 2048)].reshape(16, 128)
            return carry

        lax.fori_loop(0, 16, body, 0)
        if i == 0:
            pl.semaphore_wait(barrier, len(peers))
        swaps[i] = send(pack.at[i], got.at[i], refs["core_sem"], (i,), rel(("c", 1)))

    def group_step(i):
        loads[2 * i + 1].wait()
        swaps[i].wait_recv()
        place = i // 2

        def body(j, carry):
            jy = lax.div(j, 4)
            jz = lax.rem(j, 4) + (i % 2) * 4
            for u in range(4):
                other = got[i, pl.ds(pl.multiple_of(j * 64 + u * 16, 16), 16), :].astype(F32)
                for v in range(2):
                    at = pl.multiple_of((2 * i + 1) * GROUP + j * 8192 + u * 2048 + v * 1024, 1024)
                    row = u * 16 + v * 8
                    both = raw[:, pl.ds(at, 1024)].astype(F32).reshape(8, 128) + other[v * 8 : v * 8 + 8]
                    for p, (axes, low, rows) in enumerate(PARTS):
                        if low <= row < low + rows:
                            first, chunk = {
                                "x": (place, jy * NZ + jz),
                                "y": (jy, place * NZ + jz),
                                "z": (jz, place * NY + jy),
                            }[axes[0]]
                            at = pl.ds(pl.multiple_of(chunk * rows + row - low, 8), 8)
                            refs["sum", p][first, at, :] = both
            return carry

        lax.fori_loop(0, 16, body, 0)

    copies = {}

    def first_index(p, distance):
        a = PARTS[p][0][0]
        n = SIZES[a]
        return PLACE[distance % n] if a == "x" else lax.rem(here[a] + distance + n, n)

    def ring_step(p, d, long, k):
        axes = PARTS[p][0]
        total, slots = refs["sum", p], refs["ring", p]
        order = ring_sends(SIZES[axes[0]])
        step = 1 - 2 * d
        half = total.shape[1] // 2
        src = total.at[first_index(p, step * k), pl.ds(half_of(d, long) * half, half), :]
        if (long, k + 1) in order:
            copies[p, d, long, k + 1].wait_recv()
            landed = slots.at[d, order.index((long, k + 1))]
            add_into(landed, src, half)
            src = landed
        event = order.index((long, k))
        copies[p, d, long, k] = send(
            src, slots.at[d, event], refs["ring_sem", p], (d, event), rel((axes[0], step))
        )

    def end_step(p, d, long):
        total, slots = refs["sum", p], refs["ring", p]
        half = total.shape[1] // 2
        copies[p, d, long, 1].wait_recv()
        event = ring_sends(SIZES[PARTS[p][0][0]]).index((long, 1))
        add_into(total.at[first_index(p, 0), pl.ds(half_of(d, long) * half, half), :], slots.at[d, event], half)

    def second_index(p, distance):
        a = PARTS[p][0][1]
        return PLACE[distance % 4] if a == "x" else lax.rem(here[a] + distance, SIZES[a])

    def second_step(p):
        axes, _, rows = PARTS[p]
        size = SIZES[axes[2]] * rows
        for d in FAR_FIRST[SIZES[axes[1]]]:
            src = refs["sum", p].at[first_index(p, 0), pl.ds(pl.multiple_of(second_index(p, d) * size, 8), size), :]
            copies["two", p, d] = send(
                src, refs["two", p].at[d - 1], refs["two_sem", p], (d - 1,), rel((axes[1], d))
            )

    def third_rows(p, distance):
        axes, _, rows = PARTS[p]
        n = SIZES[axes[2]]
        base = second_index(p, 0) * (n * rows)
        return pl.ds(pl.multiple_of(base + lax.rem(here[axes[2]] + distance, n) * rows, 8), rows)

    def third_step(p):
        axes, _, rows = PARTS[p]
        size = SIZES[axes[2]] * rows
        n = SIZES[axes[1]]
        total, slots = refs["sum", p], refs["two", p]
        for d in range(1, n):
            copies["two", p, d].wait_recv()
        first = first_index(p, 0)
        for i in range(size // 32):
            at = pl.ds(pl.multiple_of(second_index(p, 0) * size + i * 32, 8), 32)
            value = total[first, at, :]
            for d in range(1, n):
                value = value + slots[d - 1, i * 32 : i * 32 + 32, :]
            total[first, at, :] = value
        for d in FAR_FIRST[SIZES[axes[2]]]:
            copies["three", p, d] = send(
                total.at[first, third_rows(p, d), :], refs["three", p].at[d - 1], refs["three_sem", p],
                (d - 1,), rel((axes[2], d)),
            )

    squares = []

    def last_step(p):
        axes, low, rows = PARTS[p]
        value = refs["sum", p][first_index(p, 0), third_rows(p, 0), :]
        for d in range(1, SIZES[axes[2]]):
            copies["three", p, d].wait_recv()
        for d in range(1, SIZES[axes[2]]):
            value = value + refs["three", p][d - 1]
        state[2, 8 + low : 8 + low + rows, :] = value
        square = value * value
        squares.extend(square[8 * q : 8 * q + 8] for q in range(rows // 8))

    def old_step():
        for copy in inputs:
            copy.wait()
        for j in range(5):
            low, high = max(16 * j - 8, 0), min(16 * j + 8, ROWS)
            state[0, 8 + low : 8 + high, :] = refs["mcode"][low:high, :].astype(F32) / 127.0 * refs["mscale"][j]
            state[1, 8 + low : 8 + high, :] = refs["vcode"][low:high, :].astype(F32) / 255.0 * refs["vscale"][j]

    did_old = False
    for task in ORDER:
        if task[0] == SECOND and not did_old:
            old_step()
            did_old = True
        kind, p = task[0], task[1]
        if kind == PACK:
            pack_step(p)
        elif kind == SUM:
            group_step(p)
        elif kind == RING:
            ring_step(p, task[2], task[3], task[4])
        elif kind == END:
            end_step(p, task[2], task[3])
        elif kind == SECOND:
            second_step(p)
        elif kind == THIRD:
            third_step(p)
        else:
            last_step(p)

    square = sum(squares[1:], squares[0])
    refs["n1"][...] = square
    norm1 = [
        send(refs["n1"], refs["n1r"].at[i], refs["norm1_sem"], (i,), rel(("x", dx), ("y", dy)))
        for i, (dx, dy) in enumerate(XY_PEERS)
    ]
    rims = [
        send(state.at[:, pl.ds(64, 8), :], state.at[:, pl.ds(0, 8), :], refs["edge_sem"], (0,), flat(1)),
        send(state.at[:, pl.ds(8, 8), :], state.at[:, pl.ds(72, 8), :], refs["edge_sem"], (1,), flat(-1)),
    ]
    for copy in norm1:
        copy.wait_recv()
    for i in range(15):
        square = square + refs["n1r"][i]
    refs["n2"][...] = square
    norm2 = [
        send(refs["n2"], refs["n2r"].at[i], refs["norm2_sem"], (i,), rel(("z", dz), ("c", dc)))
        for i, (dz, dc) in enumerate(ZC_PEERS)
    ]
    count = jnp.full((8, 128), refs["step"][0].astype(F32), F32)
    first_fix = 1.0 - jnp.exp(count * math.log(0.9))
    second_fix = 1.0 - jnp.exp(count * math.log(0.95))
    early = list(started)
    for copy in early[: -len(norm2)]:
        copy.wait_send()
    for copy in rims:
        copy.wait_recv()
    for copy in norm2:
        copy.wait_recv()
    for i in range(15):
        square = square + refs["n2r"][i]
    norm = jnp.sqrt(jnp.full((8, 128), jnp.sum(square), F32))
    clip = jnp.minimum(1.0, TOTAL**0.5 / (norm + 1e-06))

    def moments(row):
        scaled = state[2, row : row + 8, :] * clip
        momentum = 0.9 * state[0, row : row + 8, :] + 0.1 * scaled
        variance = 0.95 * state[1, row : row + 8, :] + 0.05 * scaled * scaled
        return momentum, variance

    out_ref = refs["out"]
    leaving = []

    def put(src, dst):
        copy = pltpu.make_async_copy(src, dst, refs["leave_sem"].at[len(leaving)])
        copy.start()
        leaving.append(copy)

    pairs = [moments(8 * q) for q in range(10)]
    for q in range(8):
        at = slice(8 * q, 8 * q + 8)
        momentum, variance = pairs[q + 1]
        update = momentum / first_fix / (jnp.sqrt(variance / second_fix) + 1e-08)
        out_ref[1, at, :] = update
        out_ref[0, at, :] = refs["master"][at, :] * (1.0 - 0.0001 * 0.1) - 0.0001 * update
    own_rows = pl.ds(pl.multiple_of(r * ROWS, ROWS), ROWS)
    refs["half"][...] = out_ref[0].astype(BF16)
    gathers = [
        send(refs["half"], w_ref.at[own_rows, :], refs["out_sem"], (i,), in_rep(dy, dl))
        for i, (dy, dl) in enumerate(REP_PEERS)
    ]
    put(refs["half"], w_ref.at[own_rows, :])
    put(out_ref.at[0], new_hbm)
    put(out_ref.at[1], up_hbm)
    first = (o > 0).astype(F32)
    last = (o < 255).astype(F32)
    for j in range(5):
        (ma, va), (mb, vb) = pairs[2 * j], pairs[2 * j + 1]
        ma, va, mb, vb = jnp.abs(ma), jnp.abs(va), jnp.abs(mb), jnp.abs(vb)
        if j == 0:
            ma, va = ma * first, va * first
        if j == 4:
            mb, vb = mb * last, vb * last
        m_max = jnp.max(jnp.maximum(ma, mb))
        v_max = jnp.max(jnp.maximum(va, vb))
        refs["am"][j] = m_max
        refs["av"][j] = v_max
        for q in (2 * j - 1, 2 * j):
            if 0 <= q < 8:
                at = slice(8 * q, 8 * q + 8)
                out_ref[2, at, :] = pairs[q + 1][0] / (m_max + 1e-06)
                out_ref[3, at, :] = pairs[q + 1][1] / (v_max + 1e-06)
    put(out_ref.at[2], mn_hbm)
    put(out_ref.at[3], vn_hbm)
    put(refs["am"], am_hbm)
    put(refs["av"], av_hbm)
    for copy in started[len(early) - len(norm2) :]:
        copy.wait_send()
    for copy in leaving:
        copy.wait()
    for copy in gathers:
        copy.wait_recv()


def leave(*refs):
    count = 7
    sources, results, held = refs[:count], refs[count : 2 * count], refs[2 * count : 3 * count]
    sems = refs[3 * count]
    loads = [pltpu.make_async_copy(sources[i], held[i], sems.at[0, i]) for i in range(count)]
    stores = [pltpu.make_async_copy(held[i], results[i], sems.at[1, i]) for i in range(count)]
    for copy in loads:
        copy.start()
    for load, store in zip(loads, stores):
        load.wait()
        store.start()
    for copy in stores:
        copy.wait()


def on_device(grads, momentum_codes, variance_codes, momentum_scale, variance_scale, master, step):
    hbm = pl.BlockSpec(memory_space=pl.ANY)
    tile = jax.ShapeDtypeStruct((ROWS, 128), F32)
    weights = jax.ShapeDtypeStruct((16 * ROWS, 128), BF16)
    slots = jax.ShapeDtypeStruct((5,), F32)
    shapes = (tile, weights, tile, tile, tile, slots, slots)
    results = pl.pallas_call(
        kernel,
        out_shape=shapes,
        in_specs=[hbm] * 7,
        out_specs=(hbm,) * 7,
        scratch_shapes=list(layout().values()),
        compiler_params=pltpu.CompilerParams(
            collective_id=0, has_side_effects=True, vmem_limit_bytes=48 * 2**20
        ),
        name="adam_window",
    )(
        grads, momentum_codes.reshape(ROWS, 128), variance_codes.reshape(ROWS, 128),
        momentum_scale, variance_scale, master.reshape(ROWS, 128), step,
    )
    new, weights, update, m_norm, v_norm, m_max, v_max = pl.pallas_call(
        leave,
        out_shape=shapes,
        in_specs=[hbm] * 7,
        out_specs=(hbm,) * 7,
        scratch_shapes=[pltpu.VMEM(v.shape, v.dtype) for v in shapes] + [pltpu.SemaphoreType.DMA((2, 7))],
        name="leave",
    )(*results)
    return (
        new.reshape(-1), weights.reshape(-1), update.reshape(-1), m_norm.reshape(-1), v_norm.reshape(-1), m_max, v_max
    )


def solution(mesh):
    own = P(("shard", "rep"))
    return jax.shard_map(
        on_device,
        mesh=mesh,
        in_specs=(P("shard", "rep", None), own, own, own, own, own, P()),
        out_specs=(own, P("shard"), own, own, own, own, own),
        check_vma=False,
    )
```

time: 717 us -> 71.7 us (0.10)
  waiting for transfers between devices: 541 us -> 0 us
  blocking collectives: 121 us -> 0 us
  Pallas kernels: 0 us -> 62.3 us
  other arithmetic: 20.1 us -> 0 us
  between operations: 17 us -> 1.32 us
    unnamed x4 -> x0, waiting for transfers between devices: 532 us -> none
    psum x1 -> x0, blocking collectives: 85.7 us -> none  [on_device(): norm_sq = lax.psum(jnp.sum(gsum * gsum), ('shard', 'rep'))]
    pallas_call x0 -> x2, Pallas kernels: none -> 62.3 us  [the longest x1 60.4 us: on_device(): pl.pallas_call(kernel, out_shape=shapes, in_specs=[hbm] * 7, out_specs=(h...]
    all_gather x1 -> x0, blocking collectives: 35.6 us -> none  [on_device(): lax.all_gather(new_master.astype(jnp.bfloat16), 'rep', axis=0, tiled=True)]
    convert_element_type x2 -> x0, other arithmetic: 11.5 us -> none  [the longest x1 10.8 us: on_device(): grad_terms = grads.reshape(-1).astype(jnp.float32)]
    ppermute x2 -> x0, waiting for transfers between devices: 9.13 us -> none  [the longest x1 6.84 us: extended(): lax.ppermute(lax.slice_in_dim(block, block.shape[dim] - width, None, axis...]
  transfers between devices with their start and end apart: 4 -> 0, of which waited for: 4 -> 0; matrix products, arithmetic and copies ran while one was open for 0% -> 0% of each run, Pallas kernels for 0% -> 0%
where the time goes in v3:
time: 71.7 us; the launch traced here: 71.3 us
  Pallas kernels  62.3 us (87%)
  local copies, waits for them, and re-layouts  7.74 us (11%)
  between operations  1.32 us (2%)
    pallas_call x1, Pallas kernels, on_device(): pl.pallas_call(kernel, out_shape=shapes, in_specs=[hbm] * 7, out_specs=(h...  60.4 us
    unnamed x24, local copies, waits for them, and re-layouts  7.74 us
    pallas_call x1, Pallas kernels, on_device(): pl.pallas_call(leave, out_shape=shapes, in_specs=[hbm] * 7, out_specs=(hb...  1.82 us

profile of v3, /device:TPU:1, one launch (start us, length us, event | category | flops | bytes accessed | tf_op | source)
XLA Modules:
  0.0 71.3 jit_solution(316572957932827514)
XLA Ops:
  1.3 0.0 copy-start.1
  1.3 0.7 %copy-done.1 = s32[8192]{0:T(1024)S(1)} copy-done((s32[8192]{0:T(1024)S(1)}, s32[8192]{0:T(1024)}, u32[]{:S(2)}) %copy-start.1) | copy-done | bytes 32792
  2.0 0.0 copy-start.2
  2.0 0.8 %copy-done.2 = s32[8192]{0:T(1024)S(1)} copy-done((s32[8192]{0:T(1024)S(1)}, s32[8192]{0:T(1024)}, u32[]{:S(2)}) %copy-start.2) | copy-done | bytes 32792
  2.8 0.0 copy-start.3
  2.8 0.8 %copy-done.3 = f32[8192]{0:T(1024)S(1)} copy-done((f32[8192]{0:T(1024)S(1)}, f32[8192]{0:T(1024)}, u32[]{:S(2)}) %copy-start.3) | copy-done | bytes 32792
  3.6 0.0 copy-start.8
  3.6 0.7 copy-done.8
  4.2 0.0 copy-start.9
  4.2 0.7 copy-done.9
  4.9 60.4 %adam_window.1 = (f32[64,128]{1,0:T(8,128)S(1)}, bf16[1024,128]{1,0:T(8,128)(2,1)S(1)}, f32[64,128]{1,0:T(8,128)S(1)}, f32[64,128]{1,0:T(8,128)S(1)}, f32[64,128...) custom-call(bf16[1,1,2097152]{2,1,0:T(2,128)(2,1)} %g_ref.1, s32[64,128]{1,0:T(8,128)S(1)} %bitcast.8, ...), custom_call_target="tpu_custom_call" | custom-call | tf_op jit(solution)/shard_map/adam_window/pallas_call | solution.py:455
  65.3 0.0 copy-start
  65.3 0.7 copy-done
  66.0 0.0 copy-start.4
  66.0 0.6 copy-done.4
  66.6 0.0 copy-start.5
  66.6 0.6 copy-done.5
  67.2 0.0 copy-start.6
  67.2 0.6 copy-done.6
  67.8 0.0 copy-start.7
  67.8 0.6 copy-done.7
  68.4 0.6 copy-done.10
  69.0 0.5 copy-done.11
  69.5 1.8 %leave.1 = (f32[64,128]{1,0:T(8,128)}, bf16[1024,128]{1,0:T(8,128)(2,1)}, f32[64,128]{1,0:T(8,128)}, f32[64,128]{1,0:T(8,128)}, f32[64,128]{1,0:T(8,128)}, /*index=5*/f32[5]{0:T(128)}, f32[5]{0:T(128)}) custom-call(f32[64,128]{1,0:T(8,128)} %copy-done.4, bf16[1024,128]{1,0:T(8,128)(2,1)} %copy-done, f32[64,128]{1,0:T(8,128)} %copy-done.5, ...), custom_call_target="tpu_custom_call" | custom-call | tf_op jit(solution)/shard_map/leave/pallas_call | solution.py:469
  (2 shorter events, 0.0 us)
Async XLA Ops:
  1.3 0.8 %copy-start.1 = (s32[8192]{0:T(1024)S(1)}, s32[8192]{0:T(1024)}, u32[]{:S(2)}) copy-start(s32[8192]{0:T(1024)} %param.8) | copy-start | bytes 98308
  2.0 0.8 %copy-start.2 = (s32[8192]{0:T(1024)S(1)}, s32[8192]{0:T(1024)}, u32[]{:S(2)}) copy-start(s32[8192]{0:T(1024)} %param.9) | copy-start | bytes 98308
  2.8 0.8 %copy-start.3 = (f32[8192]{0:T(1024)S(1)}, f32[8192]{0:T(1024)}, u32[]{:S(2)}) copy-start(f32[8192]{0:T(1024)} %param.12) | copy-start | bytes 98308
  3.6 0.7 copy-start.8
  4.2 0.7 copy-start.9
  65.3 0.7 copy-start
  66.0 0.6 copy-start.4
  66.6 0.6 copy-start.5
  67.2 0.6 copy-start.6
  67.8 0.6 copy-start.7
  68.4 0.6 copy-start.10
  69.0 0.5 copy-start.11

commit v4 on v3

--- a/solution.py
+++ b/solution.py
@@ -459,7 +459,7 @@
         out_specs=(hbm,) * 7,
         scratch_shapes=list(layout().values()),
         compiler_params=pltpu.CompilerParams(
-            collective_id=0, has_side_effects=True, vmem_limit_bytes=48 * 2**20
+            collective_id=0, has_side_effects=True, vmem_limit_bytes=54 * 2**20
         ),
         name="adam_window",
     )(
@@ -472,6 +472,7 @@
         in_specs=[hbm] * 7,
         out_specs=(hbm,) * 7,
         scratch_shapes=[pltpu.VMEM(v.shape, v.dtype) for v in shapes] + [pltpu.SemaphoreType.DMA((2, 7))],
+        compiler_params=pltpu.CompilerParams(vmem_limit_bytes=54 * 2**20),
         name="leave",
     )(*results)
     return (

time: 71.7 us -> 64 us (0.89)
  local copies, waits for them, and re-layouts: 7.74 us -> 0 us
    unnamed x24 -> x0, local copies, waits for them, and re-layouts: 7.74 us -> none
where the time goes in v4:
time: 64 us; the launch traced here: 63.8 us
  Pallas kernels  62.6 us (98%)
  between operations  1.29 us (2%)
    pallas_call x1, Pallas kernels, on_device(): pl.pallas_call(kernel, out_shape=shapes, in_specs=[hbm] * 7, out_specs=(h...  60.7 us
    pallas_call x1, Pallas kernels, on_device(): pl.pallas_call(leave, out_shape=shapes, in_specs=[hbm] * 7, out_specs=(hb...  1.82 us

profile of v4, /device:TPU:1, one launch (start us, length us, event | category | flops | bytes accessed | tf_op | source)
XLA Modules:
  0.0 63.8 jit_solution(13447104436478531230)
XLA Ops:
  1.3 60.7 %adam_window.1 = (f32[64,128]{1,0:T(8,128)}, bf16[1024,128]{1,0:T(8,128)(2,1)}, f32[64,128]{1,0:T(8,128)}, f32[64,128]{1,0:T(8,128)}, f32[64,128]{1,0:T(8,128)}, /*index=5*/f32[5]{0:T(128)}, f32[5]{0:T(128)}) custom-call(bf16[1,1,2097152]{2,1,0:T(2,128)(2,1)} %g_ref.1, s32[64,128]{1,0:T(8,128)} %bitcast.8, s32[64,128]{1,0:T(8,128)} %bitcast.9, f32[5]{0:T(128)} %mscale_ref.1, ...), custom_call_target="tpu_custom_call" | custom-call | tf_op jit(solution)/shard_map/adam_window/pallas_call | solution.py:455
  62.0 1.8 %leave.1 = (f32[64,128]{1,0:T(8,128)}, bf16[1024,128]{1,0:T(8,128)(2,1)}, f32[64,128]{1,0:T(8,128)}, f32[64,128]{1,0:T(8,128)}, f32[64,128]{1,0:T(8,128)}, /*index=5*/f32[5]{0:T(128)}, f32[5]{0:T(128)}) custom-call(f32[64,128]{1,0:T(8,128)} %get-tuple-element.21.refs_0_, bf16[1024,128]{1,0:T(8,128)(2,1)} %get-tuple-element.22.refs_1_, ...), custom_call_target="tpu_custom_call" | custom-call | tf_op jit(solution)/shard_map/leave/pallas_call | solution.py:469

commit v5 on v4

--- a/solution.py
+++ b/solution.py
@@ -18,7 +18,7 @@
 GROUP = 131072
 GROUP_ROWS = GROUP // 128
 
-PARTS = (("xyz", 0, 16), ("yxz", 16, 16), ("zxy", 32, 16), ("xyz", 48, 8), ("yxz", 56, 8))
+PARTS = (("zxy", 0, 16), ("xyz", 16, 16), ("yxz", 32, 16), ("xyz", 48, 8), ("yxz", 56, 8))
 
 X_OFFSETS = (2, 1, 3, 0)
 PLACE = {d: i for i, d in enumerate(X_OFFSETS)}
@@ -46,19 +46,19 @@
 PACK, SUM, RING, END, SECOND, THIRD, LAST = range(7)
 ORDER = (
     (PACK, 0), (PACK, 1), (PACK, 2), (PACK, 3), (PACK, 4), (SUM, 0), (PACK, 5), (PACK, 6), (PACK, 7), (SUM, 1),
-    (RING, 0, 0, 1, 2), (RING, 0, 1, 1, 2), (RING, 3, 0, 1, 2), (RING, 3, 1, 1, 2), (SUM, 2), (SUM, 3),
-    (RING, 0, 0, 0, 1), (RING, 1, 0, 1, 2), (RING, 1, 1, 0, 1), (RING, 2, 0, 1, 4), (RING, 2, 1, 0, 3),
-    (RING, 3, 0, 0, 1), (RING, 4, 0, 1, 2), (RING, 4, 1, 0, 1), (SUM, 4), (SUM, 5), (RING, 0, 1, 0, 1),
-    (RING, 3, 1, 0, 1), (SUM, 6), (SUM, 7), (RING, 1, 0, 0, 1), (RING, 1, 1, 1, 2), (RING, 2, 0, 0, 3),
-    (RING, 2, 1, 1, 4), (RING, 4, 0, 0, 1), (RING, 4, 1, 1, 2), (RING, 0, 0, 1, 1), (RING, 0, 1, 1, 1),
-    (RING, 2, 0, 1, 3), (RING, 2, 1, 0, 2), (RING, 3, 0, 1, 1), (RING, 1, 0, 1, 1), (RING, 3, 1, 1, 1),
-    (END, 1, 1, 0), (RING, 4, 0, 1, 1), (END, 4, 1, 0), (RING, 2, 0, 0, 2), (RING, 2, 1, 1, 3), (END, 0, 0, 0),
-    (END, 0, 1, 0), (RING, 2, 0, 1, 2), (RING, 2, 1, 0, 1), (END, 3, 0, 0), (END, 1, 0, 0), (END, 3, 1, 0),
-    (RING, 1, 1, 1, 1), (RING, 2, 0, 0, 1), (RING, 2, 1, 1, 2), (END, 4, 0, 0), (RING, 4, 1, 1, 1),
-    (RING, 2, 0, 1, 1), (END, 2, 1, 0), (END, 0, 0, 1), (END, 0, 1, 1), (SECOND, 0), (END, 3, 0, 1), (END, 1, 0, 1),
-    (END, 3, 1, 1), (SECOND, 3), (END, 2, 0, 0), (RING, 2, 1, 1, 1), (END, 1, 1, 1), (SECOND, 1), (END, 4, 0, 1),
-    (END, 2, 0, 1), (END, 4, 1, 1), (SECOND, 4), (END, 2, 1, 1), (SECOND, 2), (THIRD, 0), (THIRD, 1), (THIRD, 3),
-    (THIRD, 4), (THIRD, 2), (LAST, 0), (LAST, 2), (LAST, 1), (LAST, 3), (LAST, 4),
+    (RING, 1, 0, 1, 2), (RING, 1, 1, 1, 2), (RING, 3, 0, 1, 2), (RING, 3, 1, 1, 2), (SUM, 2), (SUM, 3),
+    (RING, 0, 0, 1, 4), (RING, 0, 1, 0, 3), (RING, 1, 0, 0, 1), (RING, 2, 0, 1, 2), (RING, 2, 1, 0, 1),
+    (RING, 3, 0, 0, 1), (RING, 4, 0, 1, 2), (RING, 4, 1, 0, 1), (SUM, 4), (SUM, 5), (RING, 1, 1, 0, 1),
+    (RING, 3, 1, 0, 1), (SUM, 6), (SUM, 7), (RING, 0, 0, 0, 3), (RING, 0, 1, 1, 4), (RING, 2, 0, 0, 1),
+    (RING, 2, 1, 1, 2), (RING, 4, 0, 0, 1), (RING, 4, 1, 1, 2), (RING, 0, 0, 1, 3), (RING, 1, 0, 1, 1),
+    (RING, 0, 1, 0, 2), (RING, 1, 1, 1, 1), (RING, 3, 0, 1, 1), (RING, 3, 1, 1, 1), (RING, 2, 0, 1, 1),
+    (END, 2, 1, 0), (RING, 0, 0, 0, 2), (RING, 0, 1, 1, 3), (RING, 4, 0, 1, 1), (END, 4, 1, 0), (RING, 0, 0, 1, 2),
+    (END, 1, 0, 0), (RING, 0, 1, 0, 1), (END, 1, 1, 0), (END, 3, 0, 0), (END, 3, 1, 0), (END, 2, 0, 0),
+    (RING, 2, 1, 1, 1), (RING, 0, 0, 0, 1), (RING, 0, 1, 1, 2), (END, 4, 0, 0), (RING, 4, 1, 1, 1),
+    (RING, 0, 0, 1, 1), (END, 0, 1, 0), (END, 1, 0, 1), (END, 1, 1, 1), (SECOND, 1), (END, 3, 0, 1), (END, 0, 0, 0),
+    (END, 3, 1, 1), (RING, 0, 1, 1, 1), (SECOND, 3), (END, 2, 0, 1), (END, 2, 1, 1), (SECOND, 2), (END, 0, 0, 1),
+    (END, 4, 0, 1), (END, 4, 1, 1), (SECOND, 4), (END, 0, 1, 1), (SECOND, 0), (THIRD, 1), (THIRD, 2), (THIRD, 3),
+    (THIRD, 4), (THIRD, 0), (LAST, 1), (LAST, 0), (LAST, 2), (LAST, 3), (LAST, 4),
 )
 
 
@@ -92,10 +92,10 @@
         "half": pltpu.VMEM((ROWS, 128), BF16),
         "am": pltpu.SMEM((5,), F32),
         "av": pltpu.SMEM((5,), F32),
-        "n1": pltpu.VMEM((8, 128), F32),
-        "n2": pltpu.VMEM((8, 128), F32),
-        "n1r": pltpu.VMEM((15, 8, 128), F32),
-        "n2r": pltpu.VMEM((15, 8, 128), F32),
+        "n1": pltpu.VMEM((1, 128), F32),
+        "n2": pltpu.VMEM((1, 128), F32),
+        "n1r": pltpu.VMEM((15, 1, 128), F32),
+        "n2r": pltpu.VMEM((15, 1, 128), F32),
         "load_sem": dma((16,)),
         "input_sem": dma((6,)),
         "core_sem": dma((2, 8)),
@@ -172,15 +172,17 @@
             load.start()
             loads.append(load)
     inputs = []
-    for i, (src, name) in enumerate(
-        (
-            (mcode_ref, "mcode"), (vcode_ref, "vcode"), (master_ref, "master"),
-            (mscale_ref, "mscale"), (vscale_ref, "vscale"), (step_ref, "step"),
-        )
-    ):
-        copy = pltpu.make_async_copy(src, refs[name], refs["input_sem"].at[i])
-        copy.start()
-        inputs.append(copy)
+
+    def input_step():
+        for i, (src, name) in enumerate(
+            (
+                (mcode_ref, "mcode"), (vcode_ref, "vcode"), (master_ref, "master"),
+                (mscale_ref, "mscale"), (vscale_ref, "vscale"), (step_ref, "step"),
+            )
+        ):
+            copy = pltpu.make_async_copy(src, refs[name], refs["input_sem"].at[i])
+            copy.start()
+            inputs.append(copy)
 
     swaps = {}
 
@@ -324,6 +326,8 @@
         kind, p = task[0], task[1]
         if kind == PACK:
             pack_step(p)
+            if p == 7:
+                input_step()
         elif kind == SUM:
             group_step(p)
         elif kind == RING:
@@ -337,7 +341,7 @@
         else:
             last_step(p)
 
-    square = sum(squares[1:], squares[0])
+    square = jnp.sum(sum(squares[1:], squares[0]), axis=0, keepdims=True)
     refs["n1"][...] = square
     norm1 = [
         send(refs["n1"], refs["n1r"].at[i], refs["norm1_sem"], (i,), rel(("x", dx), ("y", dy)))
@@ -347,6 +351,10 @@
         send(state.at[:, pl.ds(64, 8), :], state.at[:, pl.ds(0, 8), :], refs["edge_sem"], (0,), flat(1)),
         send(state.at[:, pl.ds(8, 8), :], state.at[:, pl.ds(72, 8), :], refs["edge_sem"], (1,), flat(-1)),
     ]
+    before = started[: -len(norm1) - len(rims)]
+    part = len(before) // 3
+    for copy in before[:part]:
+        copy.wait_send()
     for copy in norm1:
         copy.wait_recv()
     for i in range(15):
@@ -359,8 +367,7 @@
     count = jnp.full((8, 128), refs["step"][0].astype(F32), F32)
     first_fix = 1.0 - jnp.exp(count * math.log(0.9))
     second_fix = 1.0 - jnp.exp(count * math.log(0.95))
-    early = list(started)
-    for copy in early[: -len(norm2)]:
+    for copy in before[part : 2 * part]:
         copy.wait_send()
     for copy in rims:
         copy.wait_recv()
@@ -423,7 +430,7 @@
     put(out_ref.at[3], vn_hbm)
     put(refs["am"], am_hbm)
     put(refs["av"], av_hbm)
-    for copy in started[len(early) - len(norm2) :]:
+    for copy in before[2 * part :] + norm1 + rims + norm2 + gathers:
         copy.wait_send()
     for copy in leaving:
         copy.wait()

time: 64 us -> 62.7 us (0.980)
  Pallas kernels: 62.6 us -> 61.3 us
    pallas_call x1, Pallas kernels: 60.7 us -> 59.5 us  [on_device(): pl.pallas_call(kernel, out_shape=shapes, in_specs=[hbm] * 7, out_specs=(h...]
where the time goes in v5:
time: 62.7 us; the launch traced here: 62.6 us
  Pallas kernels  61.3 us (98%)
  between operations  1.29 us (2%)
    pallas_call x1, Pallas kernels, on_device(): pl.pallas_call(kernel, out_shape=shapes, in_specs=[hbm] * 7, out_specs=(h...  59.5 us
    pallas_call x1, Pallas kernels, on_device(): pl.pallas_call(leave, out_shape=shapes, in_specs=[hbm] * 7, out_specs=(hb...  1.82 us

profile of v5, /device:TPU:1, one launch (start us, length us, event | category | flops | bytes accessed | tf_op | source)
XLA Modules:
  0.0 62.6 jit_solution(9852823124634121950)
XLA Ops:
  1.3 59.5 %adam_window.1 = (f32[64,128]{1,0:T(8,128)}, bf16[1024,128]{1,0:T(8,128)(2,1)}, f32[64,128]{1,0:T(8,128)}, f32[64,128]{1,0:T(8,128)}, f32[64,128]{1,0:T(8,128)}, /*index=5*/f32[5]{0:T(128)}, f32[5]{0:T(128)}) custom-call(bf16[1,1,2097152]{2,1,0:T(2,128)(2,1)} %g_ref.1, s32[64,128]{1,0:T(8,128)} %bitcast.8, s32[64,128]{1,0:T(8,128)} %bitcast.9, f32[5]{0:T(128)} %mscale_ref.1, ...), custom_call_target="tpu_custom_call" | custom-call | tf_op jit(solution)/shard_map/adam_window/pallas_call | solution.py:462
  60.8 1.8 %leave.1 = (f32[64,128]{1,0:T(8,128)}, bf16[1024,128]{1,0:T(8,128)(2,1)}, f32[64,128]{1,0:T(8,128)}, f32[64,128]{1,0:T(8,128)}, f32[64,128]{1,0:T(8,128)}, /*index=5*/f32[5]{0:T(128)}, f32[5]{0:T(128)}) custom-call(f32[64,128]{1,0:T(8,128)} %get-tuple-element.21.refs_0_, bf16[1024,128]{1,0:T(8,128)(2,1)} %get-tuple-element.22.refs_1_, ...), custom_call_target="tpu_custom_call" | custom-call | tf_op jit(solution)/shard_map/leave/pallas_call | solution.py:476
